TPU v7x, 32 devices: a whole 2x2x4 slice. The times are simulated.
32 devices in a mesh: row: 8 (over z, core), col: 4 (over y, x).
Axes of the slice: x: 2, y: 2, z: 4, core: 2. Of those that a mesh axis runs over, the one named last changes fastest.
Arguments:
- left_blocks: bfloat16 [8, 4, 4, 256, 256], P('row', 'col'), may hold values from -6 to 6
- left_rows: int32 [8, 4, 4], P('row', 'col'), may hold values from 0 to 15, as said below
- left_cols: int32 [8, 4, 4], P('row', 'col'), may hold values from 0 to 31, as said below
- left_count: int32 [8, 4], P('row', 'col'), may hold values from 1 to 4, as said below
- right_blocks: bfloat16 [8, 4, 1, 256, 256], P('row', 'col'), may hold values from -0.375 to 0.375
- right_rows: int32 [8, 4, 1], P('row', 'col'), may hold values from 0 to 15, as said below
- right_cols: int32 [8, 4, 1], P('row', 'col'), may hold values from 0 to 31, as said below
- kept_rows: int32 [8, 2], P('row'), may hold values from 0 to 15, as said below
- kept_cols: int32 [4, 4], P('col'), may hold values from 0 to 31, as said below
Outputs:
- product: bfloat16 [8, 4, 2, 4, 256, 256], P('row', 'col')
Inputs may be any that keep to these rules, and one draw needn't show every extreme that they name: `left_rows`: each entry is one of the 2 entries of kept_rows for its row panel. For a slot of contraction panel k, left_cols = u * 16 + v with u 0 or 1, where v is one of the block rows that right_rows lists for sub-panel 2 * k + u (the same on every column panel). `left_count`: slots at or past the count are unused and hold arbitrary blocks and indices; some panel uses all 4 slots. `right_rows`: all column panels of one sub-panel list the same 1 distinct block rows. `right_cols`: each entry is one of the 4 entries of kept_cols for its column panel. `kept_rows`: distinct within a row panel. `kept_cols`: distinct within a column panel.
All inputs are finite; a program needn't handle non-finite values.
Results may differ from a plain program's by a relative error of at most 0.001.
Values may be sent and summed in bfloat16 or wider, within the bound.
A program may use at most 64 MiB of HBM per device.

v0:
```python
import jax
import jax.numpy as jnp
from jax import lax
from jax.sharding import PartitionSpec as P

RB = 16


def multiply_tick(totals, panel_blocks, panel_meta, window_blocks, window_meta, row_set, col_set):
    pair_count = window_meta.shape[0]
    shift_rows = (RB * jnp.arange(pair_count, dtype=jnp.int32))[:, None]
    contract = (window_meta[:, 0, :] + shift_rows).reshape(-1)
    columns = window_meta[:, 1, :].reshape(-1)
    flat_blocks = window_blocks.reshape((-1,) + window_blocks.shape[2:])
    matched = (panel_meta[1][:, None] == contract[None, :]) & (panel_meta[2][:, None] > 0)
    chosen = jnp.einsum(
        "ab,bnp->anp", matched.astype(jnp.bfloat16), flat_blocks, preferred_element_type=jnp.float32
    ).astype(jnp.bfloat16)
    picked_col = jnp.sum(jnp.where(matched, columns[None, :], 0), axis=1).astype(jnp.int32)
    slot_live = jnp.any(matched, axis=1)
    products = jnp.einsum("amn,anp->amp", panel_blocks, chosen, preferred_element_type=jnp.float32)
    row_ids = jnp.arange(row_set.shape[0], dtype=jnp.int32)
    col_ids = jnp.arange(col_set.shape[0], dtype=jnp.int32)
    row_pos = jnp.sum(
        jnp.where(panel_meta[0][:, None] == row_set[None, :], row_ids[None, :], 0), axis=1
    )
    col_pos = jnp.sum(
        jnp.where(picked_col[:, None] == col_set[None, :], col_ids[None, :], 0), axis=1
    )
    block_width = products.shape[1]
    zero_index = jnp.zeros((), jnp.int32)

    def add_slot(slot, running):
        starts = (row_pos[slot], col_pos[slot], zero_index, zero_index)
        current_block = lax.dynamic_slice(running, starts, (1, 1, block_width, block_width))
        slot_term = jnp.where(slot_live[slot], products[slot], 0.0)
        return lax.dynamic_update_slice(running, current_block + slot_term[None, None], starts)

    return lax.fori_loop(0, products.shape[0], add_slot, totals)


def body(
    left_blocks,
    left_rows,
    left_cols,
    left_count,
    right_blocks,
    right_rows,
    right_cols,
    kept_rows,
    kept_cols,
):
    panel_blocks = left_blocks[0, 0]
    slot_count = panel_blocks.shape[0]
    block_width = panel_blocks.shape[1]
    live_slot = (jnp.arange(slot_count, dtype=jnp.int32) < left_count[0, 0]).astype(jnp.int32)
    panel_meta = jnp.stack([left_rows[0, 0], left_cols[0, 0], live_slot])
    own_meta = jnp.stack([right_rows[0, 0], right_cols[0, 0]])
    row_set = kept_rows[0]
    col_set = kept_cols[0]
    totals = jnp.zeros((row_set.shape[0], col_set.shape[0], block_width, block_width), jnp.float32)
    gathered, gathered_meta = (
        lax.all_gather(right_blocks, "row", axis=0, tiled=True),
        lax.all_gather(own_meta[None, None], "row", axis=0, tiled=True),
    )
    piece_blocks = lax.all_gather(left_blocks, "col", axis=1, tiled=True)
    piece_meta = lax.all_gather(panel_meta[None, None], "col", axis=1, tiled=True)

    def one_panel(offset, partial_sum):
        window_blocks = lax.dynamic_slice_in_dim(gathered, 2 * offset, 2, 0)[:, 0]
        window_meta = lax.dynamic_slice_in_dim(gathered_meta, 2 * offset, 2, 0)[:, 0]
        return multiply_tick(
            partial_sum,
            piece_blocks[0, offset],
            piece_meta[0, offset],
            window_blocks,
            window_meta,
            row_set,
            col_set,
        )

    totals = lax.fori_loop(0, piece_blocks.shape[1], one_panel, totals)
    return totals.astype(jnp.bfloat16)[None, None]


def solution(mesh):
    in_specs = (
        P("row", "col", None, None, None),
        P("row", "col", None),
        P("row", "col", None),
        P("row", "col"),
        P("row", "col", None, None, None),
        P("row", "col", None),
        P("row", "col", None),
        P("row", None),
        P("col", None),
    )
    out_specs = P("row", "col", None, None, None, None)
    return jax.shard_map(body, mesh=mesh, in_specs=in_specs, out_specs=out_specs, check_vma=False)
```

profile of v0, /device:TPU:0, one launch (start us, length us, event | category | flops | bytes accessed | tf_op | source)
XLA Modules:
  0.0 181.7 jit_solution(5461961895133939326)
XLA Ops:
  6.5 0.7 all-gather.8.cloned.1.call-update
  7.3 0.7 all-gather.6.cloned.1.call-update
  8.7 0.7 add_bitcast_fusion
  9.4 9.5 %all-gather.2 = s32[4,3,4]{2,1,0:T(4,128)S(1)} all-gather(s32[1,3,4]{2,1,0:T(4,128)S(1)} %add_bitcast_fusion), channel_id=2, replica_groups=mesh['row'=8,'col'=4] {'col'}, dimensions={0}, use_global_device_ids=true | all-gather | bytes 240 | tf_op jit(solution)/shard_map/all_gather | solution.py:67
  20.2 1.3 dynamic-slice
  22.5 9.2 %all-reduce = s32[16]{0:T(128)S(1)} all-reduce(s32[16]{0:T(128)S(1)} %dynamic-update-slice), channel_id=3, replica_groups=mesh['row'=8,'col'=4] {'row'}, use_global_device_ids=true, to_apply=%add | all-reduce | flops 16 | bytes 128
  31.8 2.0 %all-gather.8.cloned.1.call-done = bf16[8,1,1,256,256]{4,3,2,1,0:T(8,128)(2,1)} async-done(((bf16[1,1,1,256,256]{4,3,2,1,0:T(8,128)(2,1)}), bf16[8,1,1,256,256]{4,3,2,1,0:T(8,128)(2,1)}) %all-gather.8.cloned.1.call-update) | async-done | bytes 1048592 | tf_op jit(solution)/shard_map/all_gather | solution.py:63
  33.9 36.8 %all-gather.6.cloned.1.call-done = bf16[1,4,4,256,256]{4,3,2,0,1:T(8,128)(2,1)} async-done(((bf16[1,1,4,256,256]{4,3,2,0,1:T(8,128)(2,1)}), bf16[1,4,4,256,256]{4,3,2,0,1:T(8,128)(2,1)}) %all-gather.6.cloned.1.call-update) | async-done | bytes 2097168 | tf_op jit(solution)/shard_map/all_gather | solution.py:66
  70.9 102.9 %while.37 = (s32[]{:T(128)}, f32[2,4,256,256]{3,2,1,0:T(8,128)S(1)}, s32[1,4,3,4]{3,2,1,0:T(4,128)S(1)}, s32[1,2]{1,0:T(1,128)S(1)}, s32[8,1,2,1]{2,0,3,1:T(8,12...) while((s32[]{:T(128)}, ...), condition=%wide.region_7.8_spmd, body=%wide.region_0.7_spmd.sunk | while | flops 135659648 | bytes 4195751 | solution.py:82
  71.5 1.0 constant_dynamic-slice_fusion.5
  73.0 1.3 fusion.21
  74.3 22.2 %while.38 = (s32[]{:T(128)}, f32[2,4,256,256]{3,2,1,0:T(8,128)S(1)}, s32[4]{0:T(128)S(1)}, s32[4]{0:T(128)S(1)}, pred[4]{0:T(512)(128)(4,1)S(1)}, /*index=5*/f32...) while((s32[]{:T(128)}, f32[2,4,256,256]{3,2,1,0:T(8,128)S(1)}, s32[4]{0:T(128)S(1)}, ...), condition=%wide.region_6.6_spmd, body=%wide.region_5.5_spmd.sunk | while | flops 131080 | bytes 786644 | solution.py:39
  79.3 0.6 fusion.22
  84.9 0.6 fusion.22
  90.4 0.6 fusion.22
  96.0 0.6 fusion.22
  97.2 1.0 constant_dynamic-slice_fusion.5
  98.7 1.3 fusion.21
  100.1 22.2 %while.38 = (s32[]{:T(128)}, f32[2,4,256,256]{3,2,1,0:T(8,128)S(1)}, s32[4]{0:T(128)S(1)}, s32[4]{0:T(128)S(1)}, pred[4]{0:T(512)(128)(4,1)S(1)}, /*index=5*/f32...) while((s32[]{:T(128)}, f32[2,4,256,256]{3,2,1,0:T(8,128)S(1)}, s32[4]{0:T(128)S(1)}, ...), condition=%wide.region_6.6_spmd, body=%wide.region_5.5_spmd.sunk | while | flops 131080 | bytes 786644 | solution.py:39
  105.0 0.6 fusion.22
  110.6 0.6 fusion.22
  116.2 0.6 fusion.22
  121.7 0.6 fusion.22
  123.0 1.0 constant_dynamic-slice_fusion.5
  124.5 1.3 fusion.21
  125.8 22.2 %while.38 = (s32[]{:T(128)}, f32[2,4,256,256]{3,2,1,0:T(8,128)S(1)}, s32[4]{0:T(128)S(1)}, s32[4]{0:T(128)S(1)}, pred[4]{0:T(512)(128)(4,1)S(1)}, /*index=5*/f32...) while((s32[]{:T(128)}, f32[2,4,256,256]{3,2,1,0:T(8,128)S(1)}, s32[4]{0:T(128)S(1)}, ...), condition=%wide.region_6.6_spmd, body=%wide.region_5.5_spmd.sunk | while | flops 131080 | bytes 786644 | solution.py:39
  130.8 0.6 fusion.22
  136.3 0.6 fusion.22
  148.7 1.0 constant_dynamic-slice_fusion.5
  150.2 1.3 fusion.21
  151.5 22.2 %while.38 = (s32[]{:T(128)}, f32[2,4,256,256]{3,2,1,0:T(8,128)S(1)}, s32[4]{0:T(128)S(1)}, s32[4]{0:T(128)S(1)}, pred[4]{0:T(512)(128)(4,1)S(1)}, /*index=5*/f32...) while((s32[]{:T(128)}, f32[2,4,256,256]{3,2,1,0:T(8,128)S(1)}, s32[4]{0:T(128)S(1)}, ...), condition=%wide.region_6.6_spmd, body=%wide.region_5.5_spmd.sunk | while | flops 131080 | bytes 786644 | solution.py:39
  173.8 1.1 convert_bitcast_fusion
  (106 shorter events, 35.4 us)
Async XLA Ops:
  6.5 64.3 %copy-start = (s32[1,2]{1,0:T(1,128)S(1)}, s32[1,2]{1,0:T(1,128)}, u32[]{:S(2)}) copy-start(s32[1,2]{1,0:T(1,128)} %param.20) | copy-start | bytes 28
  6.5 64.3 %copy-start.1 = (s32[1,4]{1,0:T(1,128)S(1)}, s32[1,4]{1,0:T(1,128)}, u32[]{:S(2)}) copy-start(s32[1,4]{1,0:T(1,128)} %param.21) | copy-start | bytes 52
  6.5 27.3 %all-gather.8.cloned.1.call-start = ((), (), s32[]{:S(2)}) async-start(), calls=%async_computation.1 | async-start | bytes 1179648 | tf_op jit(solution)/shard_map/all_gather | solution.py:63
  7.3 63.4 %all-gather.6.cloned.1.call-start = ((), (), s32[]{:S(2)}) async-start(), calls=%async_computation | async-start | bytes 2621440 | tf_op jit(solution)/shard_map/all_gather | solution.py:66
Sparse Core Ops, SparseCore 0:
  9.0 24.8 all-gather.7
  35.7 34.9 all-gather.5
where the time goes:
time: 183 us; the launch traced here: 182 us
  loops' own time  53 us (29%)
  waiting for transfers between devices  40.3 us (22%)
  local copies, waits for them, and re-layouts  33.2 us (18%)
  blocking collectives  18.7 us (10%)
  between operations  16.1 us (9%)
  other arithmetic  12.9 us (7%)
  matrix products  7.48 us (4%)
    another operation x4, loops' own time, multiply_tick(): return lax.fori_loop(0, products.shape[0], add_slot, totals)  52.7 us
    all_gather x1, waiting for transfers between devices, body(): piece_blocks = lax.all_gather(left_blocks, 'col', axis=1, tiled=True)  36.8 us
    dynamic_slice x32, local copies, waits for them, and re-layouts, add_slot(): starts = (row_pos[slot], col_pos[slot], zero_index, zero_index)  17.8 us
    dynamic_update_slice x16, other arithmetic, add_slot(): lax.dynamic_update_slice(running, current_block + slot_term[None, None],...  9.57 us
    all_gather x1, blocking collectives, body(): lax.all_gather(panel_meta[None, None], 'col', axis=1, tiled=True)  9.51 us
    unnamed x1, blocking collectives  9.18 us
    dynamic_slice x16, local copies, waits for them, and re-layouts, add_slot(): slot_term = jnp.where(slot_live[slot], products[slot], 0.0)  8.93 us
    dot_general x4, matrix products, multiply_tick(): jnp.einsum('amn,anp->amp', panel_blocks, chosen, preferred_element_type=j...  5.4 us
  transfers between devices with their start and end apart: 2, of which 2 were waited for; matrix products, arithmetic and copies ran while one was open for 1% of the time, Pallas kernels for 0%

commit v1 on v0

v1 whole, which is shorter than its diff:
```python
import functools

import jax
import jax.numpy as jnp
from jax import lax
from jax.experimental import pallas as pl
from jax.experimental.pallas import tpu as pltpu
from jax.sharding import PartitionSpec as P

RB = 16


def flip(index, mask):
    bit = 1
    moved = index
    while bit <= mask:
        if mask & bit:
            moved = moved + bit - 2 * bit * ((index // bit) % 2)
        bit *= 2
    return moved


def kernel(
    nr,
    nc,
    left_ref,
    lrows,
    lcols,
    lcount,
    right_ref,
    rrows,
    rcols,
    krows,
    kcols,
    out_ref,
    lefts,
    rights,
    sums,
    stage,
    meta_l,
    meta_r,
    small_l,
    small_r,
    l_send,
    l_recv,
    f_send,
    r_send,
    r_recv,
    ml_send,
    ml_recv,
    mr_send,
    mr_recv,
    own_sem,
    small_sem,
    out_sem,
):
    me_r = lax.axis_index("row")
    me_c = lax.axis_index("col")
    slots = left_ref.shape[2]
    depth = right_ref.shape[2]
    halves = nr // nc
    keep_r = krows.shape[1]
    keep_c = kcols.shape[1]

    own_left = pltpu.make_async_copy(left_ref.at[0, 0], lefts.at[me_c], own_sem.at[0])
    own_right = pltpu.make_async_copy(
        right_ref.at[0, 0], rights.at[pl.ds(me_r * depth, depth)], own_sem.at[1]
    )
    own_left.start()
    own_right.start()

    barrier = pltpu.get_barrier_semaphore()
    for p in range(1, nc):
        pl.semaphore_signal(
            barrier, inc=1, device_id={"col": flip(me_c, p)}, device_id_type=pl.DeviceIdType.MESH
        )
    for p in range(1, nr):
        pl.semaphore_signal(
            barrier, inc=1, device_id={"row": flip(me_r, p)}, device_id_type=pl.DeviceIdType.MESH
        )

    lane = lax.broadcasted_iota(jnp.int32, meta_l.shape[1:], 1)
    tile = jnp.zeros(meta_l.shape[1:], jnp.int32)
    for a in range(slots):
        tile = jnp.where(lane == a, lrows[0, 0, a], tile)
        tile = jnp.where(lane == slots + a, lcols[0, 0, a], tile)
    tile = jnp.where(lane == 2 * slots, lcount[0, 0], tile)
    base = 2 * slots + 1
    for b in range(depth):
        tile = jnp.where(lane == base + b, rrows[0, 0, b], tile)
        tile = jnp.where(lane == base + depth + b, rcols[0, 0, b], tile)
    meta_l[me_c] = tile
    meta_r[me_r] = tile
    sums[0] = jnp.zeros(sums.shape[1:], sums.dtype)

    pl.semaphore_wait(barrier, nc - 1 + nr - 1)

    def along(axis, peer, src, dst, send, recv):
        return pltpu.make_async_remote_copy(
            src_ref=src,
            dst_ref=dst,
            send_sem=send,
            recv_sem=recv,
            device_id={axis: peer},
            device_id_type=pl.DeviceIdType.MESH,
        )

    sent = []

    relayed = nc % 4 == 0
    half = slots // 2
    first = list(range(half))
    second = list(range(half, slots))
    relay_of = {1: first, 2: second}

    def send_left(p, a):
        copy = along(
            "col",
            flip(me_c, p),
            left_ref.at[0, 0, a],
            lefts.at[me_c, a],
            l_send.at[p, a],
            l_recv.at[p, a],
        )
        copy.start()
        sent.append(copy)

    if relayed:
        for a, b in zip(first + second, second + first) if len(first) == len(second) else []:
            send_left(1, a)
            send_left(2, b)
        if len(first) != len(second):
            for a in first + second:
                send_left(1, a)
            for a in second + first:
                send_left(2, a)
        direct = [p for p in range(4, nc)]
    else:
        direct = [p for p in range(1, nc)]

    def rows_of(q):
        return rights.at[pl.ds(q * depth, depth)]

    for p in [p for p in range(2, nr, 2)] + [1]:
        copy = along(
            "row",
            flip(me_r, p),
            right_ref.at[0, 0],
            rows_of(me_r),
            r_send.at[p],
            r_recv.at[p],
        )
        copy.start()
        sent.append(copy)
    for p in range(1, nr):
        copy = along(
            "row", flip(me_r, p), meta_r.at[me_r], meta_r.at[me_r], mr_send.at[p], mr_recv.at[p]
        )
        copy.start()
        sent.append(copy)
    for p in range(1, nc):
        copy = along(
            "col", flip(me_c, p), meta_l.at[me_c], meta_l.at[me_c], ml_send.at[p], ml_recv.at[p]
        )
        copy.start()
        sent.append(copy)
    for p in direct:
        for a in range(slots):
            send_left(p, a)

    def wait_left(p, a):
        k = flip(me_c, p)
        along(
            "col", k, lefts.at[k, a], lefts.at[k, a], l_send.at[p, a], l_recv.at[p, a]
        ).wait_recv()

    def wait_right(p):
        q = flip(me_r, p)
        along("row", q, rows_of(q), rows_of(q), r_send.at[p], r_recv.at[p]).wait_recv()

    waited = set()

    def pass_left(p, a):
        wait_left(p, a)
        waited.add((p, a))
        k = flip(me_c, p)
        copy = along(
            "col",
            flip(me_c, 3 - p),
            lefts.at[k, a],
            lefts.at[k, a],
            f_send.at[a],
            l_recv.at[3, a],
        )
        copy.start()
        sent.append(copy)

    def pass_right(p):
        wait_right(p)
        q = flip(me_r, p)
        copy = along("row", flip(me_r, 1), rows_of(q), rows_of(q), r_send.at[p + 1], r_recv.at[p + 1])
        copy.start()
        sent.append(copy)

    left_steps = []
    if relayed:
        for n in range(max(len(first), len(second))):
            for p in (1, 2):
                if n < len(relay_of[p]):
                    left_steps.append(functools.partial(pass_left, p, relay_of[p][n]))
    right_steps = [functools.partial(pass_right, p) for p in range(2, nr, 2)]
    while left_steps or right_steps:
        for step in left_steps[:2] + right_steps[:1]:
            step()
        left_steps, right_steps = left_steps[2:], right_steps[1:]

    for p in range(1, nr):
        q = flip(me_r, p)
        along("row", q, meta_r.at[q], meta_r.at[q], mr_send.at[p], mr_recv.at[p]).wait_recv()
    for p in range(1, nc):
        k = flip(me_c, p)
        along("col", k, meta_l.at[k], meta_l.at[k], ml_send.at[p], ml_recv.at[p]).wait_recv()
    to_small = [
        pltpu.make_async_copy(meta_l, small_l, small_sem.at[0]),
        pltpu.make_async_copy(meta_r, small_r, small_sem.at[1]),
    ]
    for copy in to_small:
        copy.start()
    for copy in to_small:
        copy.wait()

    order = [(0, a) for a in range(slots)]
    if relayed:
        order += [(1, a) for a in first] + [(2, a) for a in second]
        order += [(1, a) for a in second] + [(2, a) for a in first]
        for a, b in zip(first, second):
            order += [(3, a), (3, b)]
        order += [(3, a) for a in first[len(second) :] + second[len(first) :]]
    order += [(p, a) for p in direct for a in range(slots)]

    last = {(i, j): jnp.int32(0) for i in range(keep_r) for j in range(keep_c)}
    plan = []
    for t, (p, a) in enumerate(order):
        k = flip(me_c, p)
        row = small_l[k, 0, a]
        contract = small_l[k, 0, slots + a]
        live = a < small_l[k, 0, 2 * slots]
        source = jnp.int32(0)
        column = jnp.int32(-1)
        for u in range(halves):
            q = halves * k + u
            for b in range(depth):
                match = contract == u * RB + small_r[q, 0, base + b]
                source = jnp.where(match, q * depth + b, source)
                column = jnp.where(match, small_r[q, 0, base + depth + b], column)
        before = jnp.int32(0)
        for i in range(keep_r):
            row_on = live & (row == krows[0, i])
            for j in range(keep_c):
                on = row_on & (column == kcols[0, j])
                before = jnp.where(on, last[i, j], before)
                last[i, j] = jnp.where(on, t + 1, last[i, j])
        plan.append((k, source, before))

    own_right.wait()
    for p in [1] + [p for p in range(3, nr, 2)]:
        wait_right(p)
    own_left.wait()
    for t, (p, a) in enumerate(order):
        if p > 0 and (p, a) not in waited:
            wait_left(p, a)
        k, source, before = plan[t]
        sums[t + 1] = sums[before] + jnp.dot(
            lefts[k, a], rights[source], preferred_element_type=jnp.float32
        )

    outs = []
    for i in range(keep_r):
        for j in range(keep_c):
            stage[i, j] = sums[last[i, j]].astype(stage.dtype)
            copy = pltpu.make_async_copy(
                stage.at[i, j], out_ref.at[0, 0, i, j], out_sem.at[i * keep_c + j]
            )
            copy.start()
            outs.append(copy)
    for copy in sent:
        copy.wait_send()
    for copy in outs:
        copy.wait()


def solution(mesh):
    nr, nc = mesh.shape["row"], mesh.shape["col"]

    def body(
        left_blocks,
        left_rows,
        left_cols,
        left_count,
        right_blocks,
        right_rows,
        right_cols,
        kept_rows,
        kept_cols,
    ):
        slots, width = left_blocks.shape[2], left_blocks.shape[3]
        depth = right_blocks.shape[2]
        keep_r, keep_c = kept_rows.shape[1], kept_cols.shape[1]
        kind = left_blocks.dtype
        block = width * width
        vmem = (
            2 * block * (nc * slots + nr * depth + keep_r * keep_c)
            + 4 * block * (nc * slots + 1)
            + 4 * 1024 * (nr + nc)
            + (4 << 20)
        )
        small = pl.BlockSpec(memory_space=pltpu.SMEM)
        large = pl.BlockSpec(memory_space=pl.ANY)
        dma = pltpu.SemaphoreType.DMA
        return pl.pallas_call(
            functools.partial(kernel, nr, nc),
            out_shape=jax.ShapeDtypeStruct((1, 1, keep_r, keep_c, width, width), kind),
            in_specs=[large, small, small, small, large, small, small, small, small],
            out_specs=large,
            scratch_shapes=[
                pltpu.VMEM((nc, slots, width, width), kind),
                pltpu.VMEM((nr * depth, width, width), kind),
                pltpu.VMEM((nc * slots + 1, width, width), jnp.float32),
                pltpu.VMEM((keep_r, keep_c, width, width), kind),
                pltpu.VMEM((nc, 8, 128), jnp.int32),
                pltpu.VMEM((nr, 8, 128), jnp.int32),
                pltpu.SMEM((nc, 8, 128), jnp.int32),
                pltpu.SMEM((nr, 8, 128), jnp.int32),
                dma((nc, slots)),
                dma((nc, slots)),
                dma((slots,)),
                dma((nr,)),
                dma((nr,)),
                dma((nc,)),
                dma((nc,)),
                dma((nr,)),
                dma((nr,)),
                dma((2,)),
                dma((2,)),
                dma((keep_r * keep_c,)),
            ],
            compiler_params=pltpu.CompilerParams(
                collective_id=0, has_side_effects=True, vmem_limit_bytes=vmem
            ),
            cost_estimate=pl.CostEstimate(
                flops=2 * nc * slots * width**3, bytes_accessed=8 * block * nc * slots, transcendentals=0
            ),
        )(
            left_blocks,
            left_rows,
            left_cols,
            left_count,
            right_blocks,
            right_rows,
            right_cols,
            kept_rows,
            kept_cols,
        )

    in_specs = (
        P("row", "col", None, None, None),
        P("row", "col", None),
        P("row", "col", None),
        P("row", "col"),
        P("row", "col", None, None, None),
        P("row", "col", None),
        P("row", "col", None),
        P("row", None),
        P("col", None),
    )
    out_specs = P("row", "col", None, None, None, None)
    return jax.shard_map(body, mesh=mesh, in_specs=in_specs, out_specs=out_specs, check_vma=False)
```

time: 183 us -> 33.7 us (0.18)
  loops' own time: 53 us -> 0 us
  waiting for transfers between devices: 40.3 us -> 0 us
  local copies, waits for them, and re-layouts: 33.2 us -> 2.93 us
  Pallas kernels: 0 us -> 28.5 us
  blocking collectives: 18.7 us -> 0 us
  between operations: 16.1 us -> 2.06 us
  other arithmetic: 12.9 us -> 0 us
  matrix products: 7.48 us -> 0 us
    another operation x5 -> x0, loops' own time: 53 us -> none  [the longest x4 52.7 us: multiply_tick(): return lax.fori_loop(0, products.shape[0], add_slot, totals)]
    all_gather x2 -> x0, waiting for transfers between devices: 38.9 us -> none  [the longest x1 36.8 us: body(): piece_blocks = lax.all_gather(left_blocks, 'col', axis=1, tiled=True)]
    dynamic_slice x56 -> x0, local copies, waits for them, and re-layouts: 30.6 us -> none  [the longest x32 17.8 us: add_slot(): starts = (row_pos[slot], col_pos[slot], zero_index, zero_index)]
    pallas_call x0 -> x1, Pallas kernels: none -> 28.5 us  [body(): pl.pallas_call(functools.partial(kernel, nr, nc), out_shape=jax.ShapeDtyp...]
    dynamic_update_slice x16 -> x0, other arithmetic: 9.57 us -> none  [add_slot(): lax.dynamic_update_slice(running, current_block + slot_term[None, None],...]
    all_gather x1 -> x0, blocking collectives: 9.51 us -> none  [body(): lax.all_gather(panel_meta[None, None], 'col', axis=1, tiled=True)]
    unnamed x1 -> x0, blocking collectives: 9.18 us -> none
    dot_general x8 -> x0, matrix products: 7.48 us -> none  [the longest x4 5.4 us: multiply_tick(): jnp.einsum('amn,anp->amp', panel_blocks, chosen, preferred_element_type=j...]
  transfers between devices with their start and end apart: 2 -> 0, of which waited for: 2 -> 0; matrix products, arithmetic and copies ran while one was open for 1% -> 0% of each run, Pallas kernels for 0% -> 0%
where the time goes in v1:
time: 33.7 us; the launch traced here: 33.5 us
  Pallas kernels  28.5 us (85%)
  local copies, waits for them, and re-layouts  2.93 us (9%)
  between operations  2.06 us (6%)
    pallas_call x1, Pallas kernels, body(): pl.pallas_call(functools.partial(kernel, nr, nc), out_shape=jax.ShapeDtyp...  28.5 us
    unnamed x13, local copies, waits for them, and re-layouts  2.93 us

profile of v1, /device:TPU:0, one launch (start us, length us, event | category | flops | bytes accessed | tf_op | source)
XLA Modules:
  0.0 33.5 jit_solution(8193815557325615245)
XLA Ops:
  0.7 0.0 copy-start.5
  1.3 0.0 copy-start.2
  1.3 0.0 copy-start.3
  1.3 0.0 copy-start.4
  2.0 0.0 copy-done.5
  2.0 0.0 copy-done.2
  2.0 0.0 copy-done.3
  2.0 0.0 copy-done.4
  2.1 0.0 copy-start
  2.1 1.0 %copy-done = bf16[1,1,4,256,256]{4,3,2,1,0:T(8,128)(2,1)S(1)} copy-done((bf16[1,1,4,256,256]{4,3,2,1,0:T(8,128)(2,1)S(1)}, bf16[1,1,4,256,256]{4,3,2,1,0:T(8,128)(2,1)}, u32[]{:S(2)}) %copy-start) | copy-done | bytes 524312
  3.1 0.0 copy-start.1
  3.1 0.9 %copy-done.1 = bf16[1,1,1,256,256]{4,3,2,1,0:T(8,128)(2,1)S(1)} copy-done((bf16[1,1,1,256,256]{4,3,2,1,0:T(8,128)(2,1)S(1)}, bf16[1,1,1,256,256]{4,3,2,1,0:T(8,128)(2,1)}, u32[]{:S(2)}) %copy-start.1) | copy-done | bytes 131096
  4.0 28.5 %shard_map.91 = bf16[1,1,2,4,256,256]{5,4,3,2,1,0:T(8,128)(2,1)S(1)} custom-call(bf16[1,1,4,256,256]{4,3,2,1,0:T(8,128)(2,1)S(1)} %copy-done, s32[1,1,4]{2,1,0:T(1,128)S(1)} %copy-done.2, s32[1,1,4]{2,1,0:T(1,128)S(1)} %copy-done.3, s32[1,1]{1,0:T(1,128)S(6)} %copy.11.lcount, bf16[1,1,1,256,256]{4,3,2,1,0:T(8,128)(2,1)S(1)} %copy-done.1, ...), custom_call_target="tpu_custom_call" | custom-call | flops 536870912 | bytes 8388608 | tf_op jit(solution)/shard_map/pallas_call | solution.py:320
  32.5 1.0 %copy.14 = bf16[1,1,2,4,256,256]{5,4,3,2,1,0:T(8,128)(2,1)} copy(bf16[1,1,2,4,256,256]{5,4,3,2,1,0:T(8,128)(2,1)S(1)} %shard_map.91) | data formatting | bytes 2097152
Async XLA Ops:
  0.7 1.4 %copy-start.5 = (s32[1,4]{1,0:T(1,128)S(1)}, s32[1,4]{1,0:T(1,128)}, u32[]{:S(2)}) copy-start(s32[1,4]{1,0:T(1,128)} %kcols.1) | copy-start | bytes 52
  1.3 0.7 %copy-start.2 = (s32[1,1,4]{2,1,0:T(1,128)S(1)}, s32[1,1,4]{2,1,0:T(1,128)}, u32[]{:S(2)}) copy-start(s32[1,1,4]{2,1,0:T(1,128)} %lrows.1) | copy-start | bytes 52
  1.3 0.7 %copy-start.3 = (s32[1,1,4]{2,1,0:T(1,128)S(1)}, s32[1,1,4]{2,1,0:T(1,128)}, u32[]{:S(2)}) copy-start(s32[1,1,4]{2,1,0:T(1,128)} %lcols.1) | copy-start | bytes 52
  1.3 0.7 %copy-start.4 = (s32[1,2]{1,0:T(1,128)S(1)}, s32[1,2]{1,0:T(1,128)}, u32[]{:S(2)}) copy-start(s32[1,2]{1,0:T(1,128)} %krows.1) | copy-start | bytes 28
  2.1 1.0 %copy-start = (bf16[1,1,4,256,256]{4,3,2,1,0:T(8,128)(2,1)S(1)}, bf16[1,1,4,256,256]{4,3,2,1,0:T(8,128)(2,1)}, u32[]{:S(2)}) copy-start(bf16[1,1,4,256,256]{4,3,2,1,0:T(8,128)(2,1)} %left_ref.1) | copy-start | bytes 1572868
  3.1 0.9 %copy-start.1 = (bf16[1,1,1,256,256]{4,3,2,1,0:T(8,128)(2,1)S(1)}, bf16[1,1,1,256,256]{4,3,2,1,0:T(8,128)(2,1)}, u32[]{:S(2)}) copy-start(bf16[1,1,1,256,256]{4,3,2,1,0:T(8,128)(2,1)} %right_ref.1) | copy-start | bytes 393220

commit v2 on v1

--- a/solution.py
+++ b/solution.py
@@ -24,19 +24,25 @@
     nr,
     nc,
     left_ref,
+    lrows_ref,
+    lcols_ref,
+    lcount_ref,
+    right_ref,
+    rrows_ref,
+    rcols_ref,
+    krows_ref,
+    kcols_ref,
+    out_ref,
     lrows,
     lcols,
     lcount,
-    right_ref,
     rrows,
     rcols,
     krows,
     kcols,
-    out_ref,
     lefts,
     rights,
     sums,
-    stage,
     meta_l,
     meta_r,
     small_l,
@@ -50,9 +56,9 @@
     ml_recv,
     mr_send,
     mr_recv,
+    tiny_sem,
     own_sem,
     small_sem,
-    out_sem,
 ):
     me_r = lax.axis_index("row")
     me_c = lax.axis_index("col")
@@ -66,8 +72,22 @@
     own_right = pltpu.make_async_copy(
         right_ref.at[0, 0], rights.at[pl.ds(me_r * depth, depth)], own_sem.at[1]
     )
-    own_left.start()
-    own_right.start()
+    smalls = [
+        pltpu.make_async_copy(src, dst, tiny_sem.at[n])
+        for n, (src, dst) in enumerate(
+            (
+                (lrows_ref, lrows),
+                (lcols_ref, lcols),
+                (lcount_ref, lcount),
+                (rrows_ref, rrows),
+                (rcols_ref, rcols),
+                (krows_ref, krows),
+                (kcols_ref, kcols),
+            )
+        )
+    ]
+    for copy in smalls + [own_left, own_right]:
+        copy.start()
 
     barrier = pltpu.get_barrier_semaphore()
     for p in range(1, nc):
@@ -78,6 +98,9 @@
         pl.semaphore_signal(
             barrier, inc=1, device_id={"row": flip(me_r, p)}, device_id_type=pl.DeviceIdType.MESH
         )
+
+    for copy in smalls:
+        copy.wait()
 
     lane = lax.broadcasted_iota(jnp.int32, meta_l.shape[1:], 1)
     tile = jnp.zeros(meta_l.shape[1:], jnp.int32)
@@ -274,19 +297,11 @@
             lefts[k, a], rights[source], preferred_element_type=jnp.float32
         )
 
-    outs = []
     for i in range(keep_r):
         for j in range(keep_c):
-            stage[i, j] = sums[last[i, j]].astype(stage.dtype)
-            copy = pltpu.make_async_copy(
-                stage.at[i, j], out_ref.at[0, 0, i, j], out_sem.at[i * keep_c + j]
-            )
-            copy.start()
-            outs.append(copy)
+            out_ref[0, 0, i, j] = sums[last[i, j]].astype(out_ref.dtype)
     for copy in sent:
         copy.wait_send()
-    for copy in outs:
-        copy.wait()
 
 
 def solution(mesh):
@@ -314,19 +329,19 @@
             + 4 * 1024 * (nr + nc)
             + (4 << 20)
         )
-        small = pl.BlockSpec(memory_space=pltpu.SMEM)
-        large = pl.BlockSpec(memory_space=pl.ANY)
+        smalls = (left_rows, left_cols, left_count, right_rows, right_cols, kept_rows, kept_cols)
+        large = pl.BlockSpec(memory_space=pltpu.HBM)
         dma = pltpu.SemaphoreType.DMA
         return pl.pallas_call(
             functools.partial(kernel, nr, nc),
             out_shape=jax.ShapeDtypeStruct((1, 1, keep_r, keep_c, width, width), kind),
-            in_specs=[large, small, small, small, large, small, small, small, small],
-            out_specs=large,
-            scratch_shapes=[
+            in_specs=[large] * 9,
+            out_specs=pl.BlockSpec(memory_space=pltpu.VMEM),
+            scratch_shapes=[pltpu.SMEM(array.shape, jnp.int32) for array in smalls]
+            + [
                 pltpu.VMEM((nc, slots, width, width), kind),
                 pltpu.VMEM((nr * depth, width, width), kind),
                 pltpu.VMEM((nc * slots + 1, width, width), jnp.float32),
-                pltpu.VMEM((keep_r, keep_c, width, width), kind),
                 pltpu.VMEM((nc, 8, 128), jnp.int32),
                 pltpu.VMEM((nr, 8, 128), jnp.int32),
                 pltpu.SMEM((nc, 8, 128), jnp.int32),
@@ -340,9 +355,9 @@
                 dma((nc,)),
                 dma((nr,)),
                 dma((nr,)),
+                dma((len(smalls),)),
                 dma((2,)),
                 dma((2,)),
-                dma((keep_r * keep_c,)),
             ],
             compiler_params=pltpu.CompilerParams(
                 collective_id=0, has_side_effects=True, vmem_limit_bytes=vmem

time: 33.7 us -> 31.5 us (0.935)
  Pallas kernels: 28.5 us -> 26.3 us
    pallas_call x1, Pallas kernels: 28.5 us -> 26.3 us  [body(): pl.pallas_call(functools.partial(kernel, nr, nc), out_shape=jax.ShapeDtyp...]
where the time goes in v2:
time: 31.5 us; the launch traced here: 31.3 us
  Pallas kernels  26.3 us (83%)
  local copies, waits for them, and re-layouts  2.93 us (9%)
  between operations  2.06 us (7%)
    pallas_call x1, Pallas kernels, body(): pl.pallas_call(functools.partial(kernel, nr, nc), out_shape=jax.ShapeDtyp...  26.3 us
    unnamed x13, local copies, waits for them, and re-layouts  2.93 us

profile of v2, /device:TPU:0, one launch (start us, length us, event | category | flops | bytes accessed | tf_op | source)
XLA Modules:
  0.0 31.3 jit_solution(4068231840834403361)
XLA Ops:
  0.7 0.0 copy-start.5
  1.3 0.0 copy-start.2
  1.3 0.0 copy-start.3
  1.3 0.0 copy-start.4
  2.0 0.0 copy-done.5
  2.0 0.0 copy-done.2
  2.0 0.0 copy-done.3
  2.0 0.0 copy-done.4
  2.1 0.0 copy-start
  2.1 1.0 %copy-done = bf16[1,1,4,256,256]{4,3,2,1,0:T(8,128)(2,1)S(1)} copy-done((bf16[1,1,4,256,256]{4,3,2,1,0:T(8,128)(2,1)S(1)}, bf16[1,1,4,256,256]{4,3,2,1,0:T(8,128)(2,1)}, u32[]{:S(2)}) %copy-start) | copy-done | bytes 524312
  3.1 0.0 copy-start.1
  3.1 0.9 %copy-done.1 = bf16[1,1,1,256,256]{4,3,2,1,0:T(8,128)(2,1)S(1)} copy-done((bf16[1,1,1,256,256]{4,3,2,1,0:T(8,128)(2,1)S(1)}, bf16[1,1,1,256,256]{4,3,2,1,0:T(8,128)(2,1)}, u32[]{:S(2)}) %copy-start.1) | copy-done | bytes 131096
  4.0 26.3 %shard_map.91 = bf16[1,1,2,4,256,256]{5,4,3,2,1,0:T(8,128)(2,1)S(1)} custom-call(bf16[1,1,4,256,256]{4,3,2,1,0:T(8,128)(2,1)S(1)} %copy-done, s32[1,1,4]{2,1,0:T(1,128)S(1)} %copy-done.2, s32[1,1,4]{2,1,0:T(1,128)S(1)} %copy-done.3, s32[1,1]{1,0:T(1,128)S(6)} %copy.11.lcount_ref, bf16[1,1,1,256,256]{4,3,2,1,0:T(8,128)(2,1)S(1)} %copy-done.1, ...), custom_call_target="tpu_custom_call" | custom-call | flops 536870912 | bytes 8388608 | tf_op jit(solution)/shard_map/pallas_call | solution.py:335
  30.3 1.0 %copy.14 = bf16[1,1,2,4,256,256]{5,4,3,2,1,0:T(8,128)(2,1)} copy(bf16[1,1,2,4,256,256]{5,4,3,2,1,0:T(8,128)(2,1)S(1)} %shard_map.91) | data formatting | bytes 2097152
Async XLA Ops:
  0.7 1.4 %copy-start.5 = (s32[1,4]{1,0:T(1,128)S(1)}, s32[1,4]{1,0:T(1,128)}, u32[]{:S(2)}) copy-start(s32[1,4]{1,0:T(1,128)} %kcols_ref.1) | copy-start | bytes 52
  1.3 0.7 %copy-start.2 = (s32[1,1,4]{2,1,0:T(1,128)S(1)}, s32[1,1,4]{2,1,0:T(1,128)}, u32[]{:S(2)}) copy-start(s32[1,1,4]{2,1,0:T(1,128)} %lrows_ref.1) | copy-start | bytes 52
  1.3 0.7 %copy-start.3 = (s32[1,1,4]{2,1,0:T(1,128)S(1)}, s32[1,1,4]{2,1,0:T(1,128)}, u32[]{:S(2)}) copy-start(s32[1,1,4]{2,1,0:T(1,128)} %lcols_ref.1) | copy-start | bytes 52
  1.3 0.7 %copy-start.4 = (s32[1,2]{1,0:T(1,128)S(1)}, s32[1,2]{1,0:T(1,128)}, u32[]{:S(2)}) copy-start(s32[1,2]{1,0:T(1,128)} %krows_ref.1) | copy-start | bytes 28
  2.1 1.0 %copy-start = (bf16[1,1,4,256,256]{4,3,2,1,0:T(8,128)(2,1)S(1)}, bf16[1,1,4,256,256]{4,3,2,1,0:T(8,128)(2,1)}, u32[]{:S(2)}) copy-start(bf16[1,1,4,256,256]{4,3,2,1,0:T(8,128)(2,1)} %left_ref.1) | copy-start | bytes 1572868
  3.1 0.9 %copy-start.1 = (bf16[1,1,1,256,256]{4,3,2,1,0:T(8,128)(2,1)S(1)}, bf16[1,1,1,256,256]{4,3,2,1,0:T(8,128)(2,1)}, u32[]{:S(2)}) copy-start(bf16[1,1,1,256,256]{4,3,2,1,0:T(8,128)(2,1)} %right_ref.1) | copy-start | bytes 393220

commit v3 on v2

--- a/solution.py
+++ b/solution.py
@@ -130,6 +130,19 @@
 
     sent = []
 
+    for p in range(1, nr):
+        copy = along(
+            "row", flip(me_r, p), meta_r.at[me_r], meta_r.at[me_r], mr_send.at[p], mr_recv.at[p]
+        )
+        copy.start()
+        sent.append(copy)
+    for p in range(1, nc):
+        copy = along(
+            "col", flip(me_c, p), meta_l.at[me_c], meta_l.at[me_c], ml_send.at[p], ml_recv.at[p]
+        )
+        copy.start()
+        sent.append(copy)
+
     relayed = nc % 4 == 0
     half = slots // 2
     first = list(range(half))
@@ -172,18 +185,6 @@
             rows_of(me_r),
             r_send.at[p],
             r_recv.at[p],
-        )
-        copy.start()
-        sent.append(copy)
-    for p in range(1, nr):
-        copy = along(
-            "row", flip(me_r, p), meta_r.at[me_r], meta_r.at[me_r], mr_send.at[p], mr_recv.at[p]
-        )
-        copy.start()
-        sent.append(copy)
-    for p in range(1, nc):
-        copy = along(
-            "col", flip(me_c, p), meta_l.at[me_c], meta_l.at[me_c], ml_send.at[p], ml_recv.at[p]
         )
         copy.start()
         sent.append(copy)

time: 31.5 us -> 31.5 us (level)
  no operation moved by 1% of the time
where the time goes in v3:
time: 31.5 us; the launch traced here: 31.3 us
  Pallas kernels  26.3 us (83%)
  local copies, waits for them, and re-layouts  2.93 us (9%)
  between operations  2.06 us (7%)
    pallas_call x1, Pallas kernels, body(): pl.pallas_call(functools.partial(kernel, nr, nc), out_shape=jax.ShapeDtyp...  26.3 us
    unnamed x13, local copies, waits for them, and re-layouts  2.93 us

profile of v3, /device:TPU:0, one launch (start us, length us, event | category | flops | bytes accessed | tf_op | source)
XLA Modules:
  0.0 31.3 jit_solution(4776492553962423183)
XLA Ops:
  0.7 0.0 copy-start.5
  1.3 0.0 copy-start.2
  1.3 0.0 copy-start.3
  1.3 0.0 copy-start.4
  2.0 0.0 copy-done.5
  2.0 0.0 copy-done.2
  2.0 0.0 copy-done.3
  2.0 0.0 copy-done.4
  2.1 0.0 copy-start
  2.1 1.0 %copy-done = bf16[1,1,4,256,256]{4,3,2,1,0:T(8,128)(2,1)S(1)} copy-done((bf16[1,1,4,256,256]{4,3,2,1,0:T(8,128)(2,1)S(1)}, bf16[1,1,4,256,256]{4,3,2,1,0:T(8,128)(2,1)}, u32[]{:S(2)}) %copy-start) | copy-done | bytes 524312
  3.1 0.0 copy-start.1
  3.1 0.9 %copy-done.1 = bf16[1,1,1,256,256]{4,3,2,1,0:T(8,128)(2,1)S(1)} copy-done((bf16[1,1,1,256,256]{4,3,2,1,0:T(8,128)(2,1)S(1)}, bf16[1,1,1,256,256]{4,3,2,1,0:T(8,128)(2,1)}, u32[]{:S(2)}) %copy-start.1) | copy-done | bytes 131096
  4.0 26.3 %shard_map.91 = bf16[1,1,2,4,256,256]{5,4,3,2,1,0:T(8,128)(2,1)S(1)} custom-call(bf16[1,1,4,256,256]{4,3,2,1,0:T(8,128)(2,1)S(1)} %copy-done, s32[1,1,4]{2,1,0:T(1,128)S(1)} %copy-done.2, s32[1,1,4]{2,1,0:T(1,128)S(1)} %copy-done.3, s32[1,1]{1,0:T(1,128)S(6)} %copy.11.lcount_ref, bf16[1,1,1,256,256]{4,3,2,1,0:T(8,128)(2,1)S(1)} %copy-done.1, ...), custom_call_target="tpu_custom_call" | custom-call | flops 536870912 | bytes 8388608 | tf_op jit(solution)/shard_map/pallas_call | solution.py:336
  30.3 1.0 %copy.14 = bf16[1,1,2,4,256,256]{5,4,3,2,1,0:T(8,128)(2,1)} copy(bf16[1,1,2,4,256,256]{5,4,3,2,1,0:T(8,128)(2,1)S(1)} %shard_map.91) | data formatting | bytes 2097152
Async XLA Ops:
  0.7 1.4 %copy-start.5 = (s32[1,4]{1,0:T(1,128)S(1)}, s32[1,4]{1,0:T(1,128)}, u32[]{:S(2)}) copy-start(s32[1,4]{1,0:T(1,128)} %kcols_ref.1) | copy-start | bytes 52
  1.3 0.7 %copy-start.2 = (s32[1,1,4]{2,1,0:T(1,128)S(1)}, s32[1,1,4]{2,1,0:T(1,128)}, u32[]{:S(2)}) copy-start(s32[1,1,4]{2,1,0:T(1,128)} %lrows_ref.1) | copy-start | bytes 52
  1.3 0.7 %copy-start.3 = (s32[1,1,4]{2,1,0:T(1,128)S(1)}, s32[1,1,4]{2,1,0:T(1,128)}, u32[]{:S(2)}) copy-start(s32[1,1,4]{2,1,0:T(1,128)} %lcols_ref.1) | copy-start | bytes 52
  1.3 0.7 %copy-start.4 = (s32[1,2]{1,0:T(1,128)S(1)}, s32[1,2]{1,0:T(1,128)}, u32[]{:S(2)}) copy-start(s32[1,2]{1,0:T(1,128)} %krows_ref.1) | copy-start | bytes 28
  2.1 1.0 %copy-start = (bf16[1,1,4,256,256]{4,3,2,1,0:T(8,128)(2,1)S(1)}, bf16[1,1,4,256,256]{4,3,2,1,0:T(8,128)(2,1)}, u32[]{:S(2)}) copy-start(bf16[1,1,4,256,256]{4,3,2,1,0:T(8,128)(2,1)} %left_ref.1) | copy-start | bytes 1572868
  3.1 0.9 %copy-start.1 = (bf16[1,1,1,256,256]{4,3,2,1,0:T(8,128)(2,1)S(1)}, bf16[1,1,1,256,256]{4,3,2,1,0:T(8,128)(2,1)}, u32[]{:S(2)}) copy-start(bf16[1,1,1,256,256]{4,3,2,1,0:T(8,128)(2,1)} %right_ref.1) | copy-start | bytes 393220

commit v4 on v3

--- a/solution.py
+++ b/solution.py
@@ -68,6 +68,16 @@
     keep_r = krows.shape[1]
     keep_c = kcols.shape[1]
 
+    barrier = pltpu.get_barrier_semaphore()
+    for p in range(1, nc):
+        pl.semaphore_signal(
+            barrier, inc=1, device_id={"col": flip(me_c, p)}, device_id_type=pl.DeviceIdType.MESH
+        )
+    for p in range(1, nr):
+        pl.semaphore_signal(
+            barrier, inc=1, device_id={"row": flip(me_r, p)}, device_id_type=pl.DeviceIdType.MESH
+        )
+
     own_left = pltpu.make_async_copy(left_ref.at[0, 0], lefts.at[me_c], own_sem.at[0])
     own_right = pltpu.make_async_copy(
         right_ref.at[0, 0], rights.at[pl.ds(me_r * depth, depth)], own_sem.at[1]
@@ -86,19 +96,8 @@
             )
         )
     ]
-    for copy in smalls + [own_left, own_right]:
-        copy.start()
-
-    barrier = pltpu.get_barrier_semaphore()
-    for p in range(1, nc):
-        pl.semaphore_signal(
-            barrier, inc=1, device_id={"col": flip(me_c, p)}, device_id_type=pl.DeviceIdType.MESH
-        )
-    for p in range(1, nr):
-        pl.semaphore_signal(
-            barrier, inc=1, device_id={"row": flip(me_r, p)}, device_id_type=pl.DeviceIdType.MESH
-        )
-
+    for copy in smalls:
+        copy.start()
     for copy in smalls:
         copy.wait()
 
@@ -191,6 +190,9 @@
     for p in direct:
         for a in range(slots):
             send_left(p, a)
+
+    own_left.start()
+    own_right.start()
 
     def wait_left(p, a):
         k = flip(me_c, p)

time: 31.5 us -> 31.2 us (level)
  no operation moved by 1% of the time
where the time goes in v4:
time: 31.2 us; the launch traced here: 31 us
  Pallas kernels  26 us (83%)
  local copies, waits for them, and re-layouts  2.93 us (9%)
  between operations  2.06 us (7%)
    pallas_call x1, Pallas kernels, body(): pl.pallas_call(functools.partial(kernel, nr, nc), out_shape=jax.ShapeDtyp...  26 us
    unnamed x13, local copies, waits for them, and re-layouts  2.93 us

profile of v4, /device:TPU:0, one launch (start us, length us, event | category | flops | bytes accessed | tf_op | source)
XLA Modules:
  0.0 31.0 jit_solution(4726234514928607047)
XLA Ops:
  0.7 0.0 copy-start.5
  1.3 0.0 copy-start.2
  1.3 0.0 copy-start.3
  1.3 0.0 copy-start.4
  2.0 0.0 copy-done.5
  2.0 0.0 copy-done.2
  2.0 0.0 copy-done.3
  2.0 0.0 copy-done.4
  2.1 0.0 copy-start
  2.1 1.0 %copy-done = bf16[1,1,4,256,256]{4,3,2,1,0:T(8,128)(2,1)S(1)} copy-done((bf16[1,1,4,256,256]{4,3,2,1,0:T(8,128)(2,1)S(1)}, bf16[1,1,4,256,256]{4,3,2,1,0:T(8,128)(2,1)}, u32[]{:S(2)}) %copy-start) | copy-done | bytes 524312
  3.1 0.0 copy-start.1
  3.1 0.9 %copy-done.1 = bf16[1,1,1,256,256]{4,3,2,1,0:T(8,128)(2,1)S(1)} copy-done((bf16[1,1,1,256,256]{4,3,2,1,0:T(8,128)(2,1)S(1)}, bf16[1,1,1,256,256]{4,3,2,1,0:T(8,128)(2,1)}, u32[]{:S(2)}) %copy-start.1) | copy-done | bytes 131096
  4.0 26.0 %shard_map.91 = bf16[1,1,2,4,256,256]{5,4,3,2,1,0:T(8,128)(2,1)S(1)} custom-call(bf16[1,1,4,256,256]{4,3,2,1,0:T(8,128)(2,1)S(1)} %copy-done, s32[1,1,4]{2,1,0:T(1,128)S(1)} %copy-done.2, s32[1,1,4]{2,1,0:T(1,128)S(1)} %copy-done.3, s32[1,1]{1,0:T(1,128)S(6)} %copy.11.lcount_ref, bf16[1,1,1,256,256]{4,3,2,1,0:T(8,128)(2,1)S(1)} %copy-done.1, ...), custom_call_target="tpu_custom_call" | custom-call | flops 536870912 | bytes 8388608 | tf_op jit(solution)/shard_map/pallas_call | solution.py:338
  30.0 1.0 %copy.14 = bf16[1,1,2,4,256,256]{5,4,3,2,1,0:T(8,128)(2,1)} copy(bf16[1,1,2,4,256,256]{5,4,3,2,1,0:T(8,128)(2,1)S(1)} %shard_map.91) | data formatting | bytes 2097152
Async XLA Ops:
  0.7 1.4 %copy-start.5 = (s32[1,4]{1,0:T(1,128)S(1)}, s32[1,4]{1,0:T(1,128)}, u32[]{:S(2)}) copy-start(s32[1,4]{1,0:T(1,128)} %kcols_ref.1) | copy-start | bytes 52
  1.3 0.7 %copy-start.2 = (s32[1,1,4]{2,1,0:T(1,128)S(1)}, s32[1,1,4]{2,1,0:T(1,128)}, u32[]{:S(2)}) copy-start(s32[1,1,4]{2,1,0:T(1,128)} %lrows_ref.1) | copy-start | bytes 52
  1.3 0.7 %copy-start.3 = (s32[1,1,4]{2,1,0:T(1,128)S(1)}, s32[1,1,4]{2,1,0:T(1,128)}, u32[]{:S(2)}) copy-start(s32[1,1,4]{2,1,0:T(1,128)} %lcols_ref.1) | copy-start | bytes 52
  1.3 0.7 %copy-start.4 = (s32[1,2]{1,0:T(1,128)S(1)}, s32[1,2]{1,0:T(1,128)}, u32[]{:S(2)}) copy-start(s32[1,2]{1,0:T(1,128)} %krows_ref.1) | copy-start | bytes 28
  2.1 1.0 %copy-start = (bf16[1,1,4,256,256]{4,3,2,1,0:T(8,128)(2,1)S(1)}, bf16[1,1,4,256,256]{4,3,2,1,0:T(8,128)(2,1)}, u32[]{:S(2)}) copy-start(bf16[1,1,4,256,256]{4,3,2,1,0:T(8,128)(2,1)} %left_ref.1) | copy-start | bytes 1572868
  3.1 0.9 %copy-start.1 = (bf16[1,1,1,256,256]{4,3,2,1,0:T(8,128)(2,1)S(1)}, bf16[1,1,1,256,256]{4,3,2,1,0:T(8,128)(2,1)}, u32[]{:S(2)}) copy-start(bf16[1,1,1,256,256]{4,3,2,1,0:T(8,128)(2,1)} %right_ref.1) | copy-start | bytes 393220
